TPU v7x, 128 devices: a whole 4x4x4 slice. The times are simulated.
128 devices in a mesh: rows: 16 (over x_hi, y, core), feat: 8 (over z, x_lo).
Axes of the slice: x: 4 (x_hi: 2, x_lo: 2; x = x_hi * 2 + x_lo), y: 4, z: 4, core: 2. Of those that a mesh axis runs over, the one named last changes fastest.
Arguments:
- activations: bfloat16 [512, 96, 8192], P('rows', None, 'feat'), may hold values from -6 to 6
- out_grads: bfloat16 [512, 96, 8192], P('rows', None, 'feat'), may hold values from -6 to 6
- proj_in: bfloat16 [8192, 128], P('feat'), may hold values from -0.0625 to 0.0625
- proj_out: bfloat16 [8192, 128], P('feat'), may hold values from -0.0625 to 0.0625
- lengths: int32 [512], P('rows'), may hold values from 12 to 96
- hess_tiles: bfloat16 [16, 1024, 1024], P('feat'), may hold values from -3 to 3
- train_grads: bfloat16 [32768, 16384], P('rows', 'feat'), may hold values from -6 to 6
Outputs:
- scores: float32 [512, 32768], P('feat', 'rows')
All inputs are finite; a program needn't handle non-finite values.
Results may differ from a plain program's by a relative error of at most 0.0057.
Values may be sent and summed in bfloat16 or wider, within the bound.
A program may use at most 128 MiB of HBM per device.

v0:
```python
import jax
import jax.numpy as jnp
from jax import lax
from jax.sharding import PartitionSpec as P


def on_device(activations, out_grads, proj_in, proj_out, lengths, hess_tiles, train_grads):
    queries, seqlen, local_width = activations.shape
    rank = proj_in.shape[1]
    act_part = jnp.dot(
        activations.reshape(queries * seqlen, local_width),
        proj_in,
        preferred_element_type=jnp.float32,
    )
    grad_part = jnp.dot(
        out_grads.reshape(queries * seqlen, local_width),
        proj_out,
        preferred_element_type=jnp.float32,
    )
    act_sum, grad_sum = lax.psum((act_part, grad_part), "feat")
    share_width = rank // lax.axis_size("feat")
    grad_share = lax.dynamic_slice_in_dim(
        grad_sum, lax.axis_index("feat") * share_width, share_width, 1
    )
    positions = jnp.arange(seqlen, dtype=jnp.int32)
    keep_mask = (
        (positions[None, :] < lengths[:, None]).astype(jnp.float32).reshape(queries * seqlen, 1)
    )
    act_low = (act_sum * keep_mask).astype(jnp.bfloat16).reshape(queries, seqlen, rank)
    grad_low = (grad_share * keep_mask).astype(jnp.bfloat16).reshape(queries, seqlen, -1)
    kron = jnp.einsum("qti,qtj->qij", grad_low, act_low, preferred_element_type=jnp.float32)
    kron = (kron * (1.0 / jnp.sqrt(jnp.float32(seqlen)))).astype(jnp.bfloat16)
    blocks_here = hess_tiles.shape[0]
    block_order = hess_tiles.shape[1]
    kron_blocks = kron.reshape(queries, blocks_here, block_order)
    precond = jnp.einsum(
        "qbk,bkl->qbl", kron_blocks, hess_tiles, preferred_element_type=jnp.float32
    )
    precond = precond.astype(jnp.bfloat16).reshape(queries, blocks_here * block_order)
    partial_scores = lax.dot_general(
        lax.all_gather(precond, "rows", axis=0, tiled=True),
        train_grads,
        (((1,), (1,)), ((), ())),
        preferred_element_type=jnp.float32,
    )
    summed = lax.psum_scatter(partial_scores, "feat", scatter_dimension=0, tiled=True)
    return summed * (1.0 / rank)


def solution(mesh):
    return jax.shard_map(
        on_device,
        mesh=mesh,
        in_specs=(
            P("rows", None, "feat"),
            P("rows", None, "feat"),
            P("feat", None),
            P("feat", None),
            P("rows"),
            P("feat", None, None),
            P("rows", "feat"),
        ),
        out_specs=P("feat", "rows"),
        check_vma=False,
    )
```

profile of v0, /device:TPU:1, one launch (start us, length us, event | category | flops | bytes accessed | tf_op | source)
XLA Modules:
  0.0 328.1 jit_solution(14449940982368767366)
XLA Ops:
  6.5 0.0 copy-start
  6.5 0.0 all-reduce.3.cloned.1.call-start
  6.5 0.9 copy-done
  7.5 0.0 copy-start.1
  7.5 0.0 copy-start.2
  7.5 5.9 %fusion.6 = f32[3072,128]{1,0:T(8,128)} fusion(bf16[3072,1024]{1,0:T(8,128)(2,1)} %bitcast.18, bf16[1024,128]{1,0:T(8,128)(2,1)S(1)} %copy-done), kind=kOutput, calls=%fused_computation.12 | convolution fusion | flops 805306368 | bytes 8126464 | tf_op jit(solution)/shard_map/dot_general | solution.py:10
  13.4 0.0 copy-done.1
  13.4 0.0 copy-done.2
  13.4 0.0 copy-start.3
  13.4 3.4 %fusion.5 = f32[3072,128]{0,1:T(8,128)} fusion(bf16[3072,1024]{1,0:T(8,128)(2,1)S(1)} %bitcast.17, bf16[1024,128]{1,0:T(8,128)(2,1)S(1)} %copy-done.2), kind=kOutput, calls=%fused_computation.11 | convolution fusion | flops 805306368 | bytes 8126464 | tf_op jit(solution)/shard_map/dot_general | solution.py:15
  16.8 0.0 all-reduce.3.cloned.1.call-update
  16.8 0.0 all-gather.2.cloned.1.call-start
  16.8 0.0 copy-done.3
  16.8 0.1 fusion.4
  16.9 0.1 reshape.43
  17.0 147.6 %all-reduce.3.cloned.1.call-done = (f32[3072,128]{1,0:T(8,128)}, f32[3072,128]{0,1:T(8,128)}) async-done(((f32[3072,128]{1,0:T(8,128)}, f32[3072,128]{0,1:T(8,128)}), (f32[3072,128]{1,0:T(8,128)}, f32[3072,128]{0,1:T(8,128)})) %all-reduce.3.cloned.1.call-update) | async-done | bytes 3145744 | tf_op jit(solution)/shard_map/psum | solution.py:20
  164.6 1.9 multiply_convert_fusion
  166.5 1.0 multiply_convert_fusion.1
  167.4 0.2 reshape.38
  167.6 0.3 fusion
  167.9 3.0 fusion.1
  171.0 0.7 copy.13
  171.6 0.0 all-gather.2.cloned.1.call-update
  171.7 0.0 reduce-scatter.2.cloned.1.call-start
  171.7 47.7 %all-gather.2.cloned.1.call-done = bf16[512,2048]{1,0:T(8,128)(2,1)} async-done(((bf16[32,2048]{1,0:T(8,128)(2,1)}), bf16[512,2048]{1,0:T(8,128)(2,1)}) %all-gather.2.cloned.1.call-update) | async-done | bytes 2097168 | tf_op jit(solution)/shard_map/all_gather | solution.py:41
  219.4 10.5 %fusion.7 = f32[512,2048]{1,0:T(8,128)} fusion(bf16[512,2048]{1,0:T(8,128)(2,1)} %all-gather.2.cloned.1.call-done, bf16[2048,2048]{1,0:T(8,128)(2,1)} %param.13), kind=kOutput, calls=%fused_computation.13 | convolution fusion | flops 4294967296 | bytes 14680064 | tf_op jit(solution)/shard_map/dot_general | solution.py:40
  229.9 0.0 reduce-scatter.2.cloned.1.call-update
  229.9 89.8 %reduce-scatter.2.cloned.1.call-done = f32[64,2048]{1,0:T(8,128)} async-done(((f32[512,2048]{1,0:T(8,128)}), f32[64,2048]{1,0:T(8,128)}) %reduce-scatter.2.cloned.1.call-update) | async-done | bytes 524304 | tf_op jit(solution)/shard_map/reduce_scatter | solution.py:46
  319.7 1.9 broadcast_multiply_fusion
  (1 shorter events, 0.0 us)
Async XLA Ops:
  6.5 1.0 copy-start
  6.5 158.0 %all-reduce.3.cloned.1.call-start = ((), (), s32[]{:S(2)}) async-start(), calls=%async_computation.3 | async-start | bytes 6291456 | tf_op jit(solution)/shard_map/psum | solution.py:20
  7.5 5.9 %copy-start.1 = (bf16[32,96,1024]{2,1,0:T(8,128)(2,1)S(1)}, bf16[32,96,1024]{2,1,0:T(8,128)(2,1)}, u32[]{:S(2)}) copy-start(bf16[32,96,1024]{2,1,0:T(8,128)(2,1)} %param.8) | copy-start | bytes 18874372
  7.5 5.9 %copy-start.2 = (bf16[1024,128]{1,0:T(8,128)(2,1)S(1)}, bf16[1024,128]{1,0:T(8,128)(2,1)}, u32[]{:S(2)}) copy-start(bf16[1024,128]{1,0:T(8,128)(2,1)} %param.10) | copy-start | bytes 786436
  13.4 3.5 %copy-start.3 = (s32[32]{0:T(128)S(1)}, s32[32]{0:T(128)}, u32[]{:S(2)}) copy-start(s32[32]{0:T(128)} %param.11) | copy-start | bytes 388
  16.8 202.6 %all-gather.2.cloned.1.call-start = ((), (), s32[]{:S(2)}) async-start(), calls=%async_computation.1 | async-start | bytes 2228224 | tf_op jit(solution)/shard_map/all_gather | solution.py:41
  171.7 148.1 %reduce-scatter.2.cloned.1.call-start = ((), (), s32[]{:S(2)}) async-start(), calls=%async_computation.2 | async-start | bytes 4718592 | tf_op jit(solution)/shard_map/reduce_scatter | solution.py:46
Sparse Core Ops, SparseCore 0:
  16.9 147.6 all-reduce.2
  171.8 47.5 all-gather.1
  230.0 89.6 reduce-scatter.1
where the time goes:
time: 328 us
  waiting for transfers between devices  285 us (87%)
  matrix products  23.1 us (7%)
  between operations  13.1 us (4%)
  other arithmetic  4.77 us (1%)
    psum x1, waiting for transfers between devices, on_device(): act_sum, grad_sum = lax.psum((act_part, grad_part), 'feat')  148 us
    reduce_scatter x1, waiting for transfers between devices, on_device(): lax.psum_scatter(partial_scores, 'feat', scatter_dimension=0, tiled=True)  89.8 us
    all_gather x1, waiting for transfers between devices, on_device(): lax.all_gather(precond, 'rows', axis=0, tiled=True)  47.7 us
    dot_general x1, matrix products, on_device(): lax.dot_general(lax.all_gather(precond, 'rows', axis=0, tiled=True), trai...  10.5 us
  transfers between devices with their start and end apart: 3, of which 3 were waited for; matrix products, arithmetic and copies ran while one was open for 0% of the time, Pallas kernels for 0%

commit v1 on v0

v1 whole, which is shorter than its diff:
```python
import jax
import jax.numpy as jnp
from jax import lax
from jax.experimental import pallas as pl
from jax.experimental.pallas import tpu as pltpu
from jax.sharding import PartitionSpec as P

MESH = pl.DeviceIdType.MESH
BF16 = jnp.bfloat16
F32 = jnp.float32
WAVES = 2
FEAT_PEERS = [(dz, dx) for dx in (1, 0) for dz in (2, 1, 3, 0) if (dz, dx) != (0, 0)]
ROW_PEERS = [(dx, dy) for dx in (1, 0) for dy in (2, 1, 3, 0) if (dx, dy) != (0, 0)]


def kernel(
    act, grad, proj_in, proj_out, lengths, hess, train, out,
    act_v, grad_v, pin_v, pout_v, hess_v, train_v,
    part_send, part_recv, part_own,
    kron_send, kron_recv, kron_f32, kron_lhs,
    gathered, score_f32, score_send, score_recv,
    load_sem, part_ss, part_rs, kron_ss, kron_rs,
    row_ss, row_rs, core_ss, core_rs, score_ss, score_rs,
):
    r = lax.axis_index("rows")
    f = lax.axis_index("feat")
    xh, y, c = r // 8, (r // 2) % 4, r % 2
    z, xl = f // 2, f % 2

    def feat_at(dz, dx):
        return lax.rem(z + dz, 4) * 2 + lax.rem(xl + dx, 2)

    def rows_at(dx, dy):
        return lax.rem(xh + dx, 2) * 8 + lax.rem(y + dy, 4) * 2 + c

    other_core = (r - c + (1 - c), f)

    loads = {}

    def load(key, src, dst, sem):
        loads[key] = pltpu.make_async_copy(src, dst, load_sem.at[sem])
        loads[key].start()

    load("pin", proj_in, pin_v, 0)
    load("pout", proj_out, pout_v, 1)
    barrier = pltpu.get_barrier_semaphore()
    targets = [(r, feat_at(*p)) for p in FEAT_PEERS]
    targets += [(rows_at(*p), f) for p in ROW_PEERS] + [other_core]
    for target in targets:
        pl.semaphore_signal(barrier, 1, device_id=target, device_id_type=MESH)
    sem = 4
    for w in range(WAVES):
        for k, p in enumerate(FEAT_PEERS + [(0, 0)]):
            row = pl.multiple_of((w * 16 + feat_at(*p) * 2) * 96, 192)
            load(("act", w, k), act.at[pl.ds(row, 192)], act_v.at[w, k], sem)
            load(("grad", w, k), grad.at[pl.ds(row, 192)], grad_v.at[w, k], sem + 1)
            sem += 2

    part_copies = {}
    for w in range(WAVES):
        for k, p in enumerate(FEAT_PEERS + [(0, 0)]):
            if w == 0 and k == 0:
                loads["pin"].wait()
                loads["pout"].wait()
            loads["act", w, k].wait()
            loads["grad", w, k].wait()
            a = jnp.dot(act_v[w, k], pin_v[...], preferred_element_type=F32)
            g = jnp.dot(grad_v[w, k], pout_v[...], preferred_element_type=F32)
            if k == len(FEAT_PEERS):
                part_own[w, :, 0:128] = a
                part_own[w, :, 128:256] = g
            else:
                part_send[w, k, :, 0:128] = a.astype(BF16)
                part_send[w, k, :, 128:256] = g.astype(BF16)
                if w == 0 and k == 0:
                    pl.semaphore_wait(barrier, len(targets))
                copy = pltpu.make_async_remote_copy(
                    part_send.at[w, k], part_recv.at[w, k],
                    part_ss.at[w, k], part_rs.at[w, k],
                    device_id=(r, feat_at(*p)), device_id_type=MESH,
                )
                if w > 0:
                    part_copies[w - 1, k].wait_send()
                copy.start()
                part_copies[w, k] = copy
        if w == 0:
            load("hess", hess, hess_v, 2)
    load("train", train, train_v, 3)

    n_feat = len(FEAT_PEERS)
    n_row = len(ROW_PEERS)
    sends = []

    def kron_stage(w):
        for k in range(n_feat):
            part_copies[w, k].wait_recv()
        total = part_own[w]
        for k in range(n_feat):
            total = total + part_recv[w, k].astype(F32)
        token = lax.broadcasted_iota(jnp.int32, (96, 256), 0)
        for q in range(2):
            length = lengths[w * 16 + f * 2 + q]
            both = jnp.where(token < length, total[q * 96:(q + 1) * 96], 0.0).astype(BF16)
            kron = lax.dot_general(
                both[:, 128:256], both[:, 0:128], (((0,), (0,)), ((), ())),
                preferred_element_type=F32,
            )
            kron = kron * (1.0 / jnp.sqrt(jnp.float32(96)))
            kron_send[w, :, q * 128:(q + 1) * 128] = kron.astype(BF16)
        copies = []
        for k, p in enumerate(FEAT_PEERS):
            target = feat_at(*p)
            copy = pltpu.make_async_remote_copy(
                kron_send.at[w, pl.ds(pl.multiple_of(target * 16, 16), 16)], kron_recv.at[w, f],
                kron_ss.at[w, k], kron_rs.at[w, k],
                device_id=(r, target), device_id_type=MESH,
            )
            copy.start()
            copies.append(copy)
        kron_recv[w, f] = kron_send[w, pl.ds(pl.multiple_of(f * 16, 16), 16)]
        return copies

    def precond_stage(w, copies):
        for copy in copies:
            copy.wait_recv()
            sends.append(copy)
        if w == 0:
            loads["hess"].wait()
        for s in range(8):
            for q in range(2):
                kron_f32[pl.ds((s * 2 + q) * 16, 16), :] = (
                    kron_recv[w, s, :, q * 128:(q + 1) * 128].astype(F32)
                )
        for i in range(16):
            kron_lhs[:, i * 128:(i + 1) * 128] = (
                kron_f32[pl.ds(i, 16, stride=16), :].astype(BF16)
            )
        for b in range(2):
            gathered[w, r, :, b * 1024:(b + 1) * 1024] = jnp.dot(
                kron_lhs[:, b * 1024:(b + 1) * 1024], hess_v[b], preferred_element_type=F32
            ).astype(BF16)
        copies = []
        for k, p in enumerate(ROW_PEERS):
            copy = pltpu.make_async_remote_copy(
                gathered.at[w, r], gathered.at[w, r], row_ss.at[w, k], row_rs.at[w, k],
                device_id=(rows_at(*p), f), device_id_type=MESH,
            )
            copy.start()
            copies.append(copy)
        return copies

    def forward(w, k, block):
        copy = pltpu.make_async_remote_copy(
            gathered.at[w, block], gathered.at[w, block], core_ss.at[w, k], core_rs.at[w, k],
            device_id=other_core, device_id_type=MESH,
        )
        copy.start()
        return copy

    def gather_stage(w, copies):
        forwards = [forward(w, n_row, r)]
        for k in (6, 4, 5, 2, 3, 1, 0):
            dx, dy = ROW_PEERS[k]
            copies[k].wait_recv()
            forwards.append(forward(w, k, rows_at(2 - dx, 4 - dy)))
        for copy in forwards:
            copy.wait_recv()
        sends.extend(copies)
        sends.extend(forwards)

    def score_stage(w):
        copies = []
        if w == 0:
            loads["train"].wait()
        for h in range(2):

            @pl.loop(0, 4)
            def _(n):
                col = pl.multiple_of(n * 256, 256)
                acc = lax.dot_general(
                    gathered[w].reshape(256, 2048),
                    train_v[pl.ds(pl.multiple_of(h * 1024 + col, 256), 256), :],
                    (((1,), (1,)), ((), ())), preferred_element_type=F32,
                )
                score_f32[w, h, :, pl.ds(col, 256)] = acc
                score_send[w, h, :, pl.ds(col, 256)] = acc.astype(BF16)

            for k, p in enumerate(FEAT_PEERS):
                target = feat_at(*p)
                copy = pltpu.make_async_remote_copy(
                    score_send.at[w, h, pl.ds(pl.multiple_of(target * 32, 32), 32)],
                    score_recv.at[w, h, k],
                    score_ss.at[w, h, k], score_rs.at[w, h, k],
                    device_id=(r, target), device_id_type=MESH,
                )
                copy.start()
                copies.append(copy)
        return copies

    def final_stage(w, copies):
        for h in range(2):
            for copy in copies[h * n_feat:(h + 1) * n_feat]:
                copy.wait_recv()
            total = score_f32[w, h, pl.ds(pl.multiple_of(f * 32, 32), 32), :]
            for k in range(n_feat):
                total = total + score_recv[w, h, k].astype(F32)
            total = total * (1.0 / 128)
            for core in range(2):
                out[pl.ds(core * 32 + w * 16, 16), pl.ds(h * 1024, 1024)] = (
                    total[core * 16:(core + 1) * 16]
                )
        sends.extend(copies)

    k0 = kron_stage(0)
    p0 = precond_stage(0, k0)
    gather_stage(0, p0)
    s0 = score_stage(0)
    k1 = kron_stage(1)
    p1 = precond_stage(1, k1)
    gather_stage(1, p1)
    s1 = score_stage(1)
    final_stage(0, s0)
    final_stage(1, s1)
    for k in range(n_feat):
        part_copies[WAVES - 1, k].wait_send()
    for copy in sends:
        copy.wait_send()


def on_device(activations, out_grads, proj_in, proj_out, lengths, hess_tiles, train_grads):
    hbm = pl.BlockSpec(memory_space=pl.ANY)
    n_feat, n_row = len(FEAT_PEERS), len(ROW_PEERS)
    dma = pltpu.SemaphoreType.DMA
    return pl.pallas_call(
        kernel,
        out_shape=jax.ShapeDtypeStruct((64, 2048), F32),
        in_specs=[hbm, hbm, hbm, hbm, pl.BlockSpec(memory_space=pltpu.SMEM), hbm, hbm],
        out_specs=pl.BlockSpec(memory_space=pltpu.VMEM),
        scratch_shapes=[
            pltpu.VMEM((WAVES, 8, 192, 1024), BF16),
            pltpu.VMEM((WAVES, 8, 192, 1024), BF16),
            pltpu.VMEM((1024, 128), BF16),
            pltpu.VMEM((1024, 128), BF16),
            pltpu.VMEM((2, 1024, 1024), BF16),
            pltpu.VMEM((2048, 2048), BF16),
            pltpu.VMEM((WAVES, n_feat, 192, 256), BF16),
            pltpu.VMEM((WAVES, n_feat, 192, 256), BF16),
            pltpu.VMEM((WAVES, 192, 256), F32),
            pltpu.VMEM((WAVES, 128, 256), BF16),
            pltpu.VMEM((WAVES, 8, 16, 256), BF16),
            pltpu.VMEM((256, 128), F32),
            pltpu.VMEM((16, 2048), BF16),
            pltpu.VMEM((WAVES, 16, 16, 2048), BF16),
            pltpu.VMEM((WAVES, 2, 256, 1024), F32),
            pltpu.VMEM((WAVES, 2, 256, 1024), BF16),
            pltpu.VMEM((WAVES, 2, n_feat, 32, 1024), BF16),
            dma((4 + WAVES * 16,)),
            dma((WAVES, n_feat)), dma((WAVES, n_feat)),
            dma((WAVES, n_feat)), dma((WAVES, n_feat)),
            dma((WAVES, n_row)), dma((WAVES, n_row)),
            dma((WAVES, n_row + 1)), dma((WAVES, n_row + 1)),
            dma((WAVES, 2, n_feat)), dma((WAVES, 2, n_feat)),
        ],
        compiler_params=pltpu.CompilerParams(
            collective_id=0, has_side_effects=True, vmem_limit_bytes=56 * 1024 * 1024
        ),
        cost_estimate=pl.CostEstimate(
            flops=6_000_000_000, bytes_accessed=26_000_000, transcendentals=0
        ),
        name="influence",
    )(
        activations.reshape(3072, 1024), out_grads.reshape(3072, 1024),
        proj_in, proj_out, lengths, hess_tiles, train_grads,
    )


def solution(mesh):
    return jax.shard_map(
        on_device,
        mesh=mesh,
        in_specs=(
            P("rows", None, "feat"),
            P("rows", None, "feat"),
            P("feat", None),
            P("feat", None),
            P("rows"),
            P("feat", None, None),
            P("rows", "feat"),
        ),
        out_specs=P("feat", "rows"),
        check_vma=False,
    )
```

time: 328 us -> 87.3 us (0.27)
  waiting for transfers between devices: 285 us -> 0 us
  Pallas kernels: 0 us -> 85.3 us
  matrix products: 23.1 us -> 0 us
  between operations: 13.1 us -> 0.01 us
  other arithmetic: 4.77 us -> 0 us
    psum x1 -> x0, waiting for transfers between devices: 148 us -> none  [on_device(): act_sum, grad_sum = lax.psum((act_part, grad_part), 'feat')]
    reduce_scatter x1 -> x0, waiting for transfers between devices: 89.8 us -> none  [on_device(): lax.psum_scatter(partial_scores, 'feat', scatter_dimension=0, tiled=True)]
    pallas_call x0 -> x1, Pallas kernels: none -> 85.3 us  [on_device(): pl.pallas_call(kernel, out_shape=jax.ShapeDtypeStruct((64, 2048), F32), i...]
    all_gather x1 -> x0, waiting for transfers between devices: 47.7 us -> none  [on_device(): lax.all_gather(precond, 'rows', axis=0, tiled=True)]
    dot_general x5 -> x0, matrix products: 23.1 us -> none  [the longest x1 10.5 us: on_device(): lax.dot_general(lax.all_gather(precond, 'rows', axis=0, tiled=True), trai...]
  transfers between devices with their start and end apart: 3 -> 0, of which waited for: 3 -> 0; matrix products, arithmetic and copies ran while one was open for 0% -> 0% of each run, Pallas kernels for 0% -> 0%
where the time goes in v1:
time: 87.3 us; the launch traced here: 87.2 us
  Pallas kernels  85.3 us (98%)
  local copies, waits for them, and re-layouts  1.87 us (2%)
    pallas_call x1, Pallas kernels, on_device(): pl.pallas_call(kernel, out_shape=jax.ShapeDtypeStruct((64, 2048), F32), i...  85.3 us
    unnamed x1, local copies, waits for them, and re-layouts  1.87 us

profile of v1, /device:TPU:1, one launch (start us, length us, event | category | flops | bytes accessed | tf_op | source)
XLA Modules:
  0.0 87.2 jit_solution(10859590351886486300)
XLA Ops:
  0.0 85.3 %influence.1 = f32[64,2048]{1,0:T(8,128)} custom-call(bf16[3072,1024]{1,0:T(8,128)(2,1)} %bitcast.2, bf16[3072,1024]{1,0:T(8,128)(2,1)} %bitcast.3, bf16[1024,128]{1,0:T(8,128)(2,1)} %proj_in.1, bf16[1024,128]{1,0:T(8,128)(2,1)} %proj_out.1, s32[32]{0:T(128)} %lengths.1, bf16[2,1024,1024]{2,1,0:T(8,128)(2,1)} %hess.1, bf16[2048,2048]{1,0:T(8,128)(2,1)} %train.1), custom_call_target="tpu_custom_call" | custom-call | flops 6000000000 | bytes 26000000 | tf_op jit(solution)/shard_map/influence/pallas_call | solution.py:234
  85.3 1.9 %copy.9 = f32[64,2048]{1,0:T(8,128)} copy(f32[64,2048]{1,0:T(8,128)} %influence.1) | data formatting | bytes 1048576

commit v2 on v1

v2 whole, which is shorter than its diff:
```python
import jax
import jax.numpy as jnp
from jax import lax
from jax.experimental import pallas as pl
from jax.experimental.pallas import tpu as pltpu
from jax.sharding import PartitionSpec as P

MESH = pl.DeviceIdType.MESH
BF16 = jnp.bfloat16
F32 = jnp.float32
WAVES = 2
NTILE = 512
FEAT_PEERS = [(dz, dx) for dx in (1, 0) for dz in (2, 1, 3, 0) if (dz, dx) != (0, 0)]
ROW_PEERS = [(dx, dy) for dx in (1, 0) for dy in (2, 1, 3, 0) if (dx, dy) != (0, 0)]
PART_ORDER = [
    ("grad", 2, 0), ("grad", 2, 1), ("act", 2, 1), ("grad", 1, 0), ("grad", 1, 1), ("act", 1, 1),
    ("grad", 3, 0), ("grad", 3, 1), ("act", 3, 1), ("act", 0, 1),
    ("grad", 0, 1), ("act", 2, 0), ("act", 1, 0), ("act", 3, 0), ("grad", 0, 0), ("act", 0, 0),
]


def kernel(
    act, grad, proj_in, proj_out, lengths_hbm, hess, train, out,
    lengths,
    act_v, grad_v, pin_v, pout_v, hess_v, train_v,
    a_send, a_recv, a_own, a_sum, a_recv2,
    g_send, g_recv, g_own, g_sum, g_recv2,
    kron_send, kron_recv, kron_f32, kron_lhs,
    gathered, score_f32, score_send, x_recv, x_sum, x_recv2, z_recv, z_sum, z_recv2,
    load_sem, a_ss, a_rs, g_ss, g_rs, kron_ss, kron_rs,
    row_ss, row_rs, core_ss, core_rs, xs_ss, xs_rs, zs_ss, zs_rs,
):
    r = lax.axis_index("rows")
    f = lax.axis_index("feat")
    xh, y, c = r // 8, (r // 2) % 4, r % 2
    z, xl = f // 2, f % 2

    def feat_at(dz, dx):
        return lax.rem(z + dz, 4) * 2 + lax.rem(xl + dx, 2)

    def rows_at(dx, dy):
        return lax.rem(xh + dx, 2) * 8 + lax.rem(y + dy, 4) * 2 + c

    other_core = (r - c + (1 - c), f)
    sends = []

    def send(src, dst, ssem, rsem, target):
        copy = pltpu.make_async_remote_copy(
            src, dst, ssem, rsem, device_id=target, device_id_type=MESH
        )
        copy.start()
        sends.append(copy)
        return copy

    loads = {}

    def load(key, src, dst, sem):
        loads[key] = pltpu.make_async_copy(src, dst, load_sem.at[sem])
        loads[key].start()

    load("pin", proj_in, pin_v, 0)
    load("pout", proj_out, pout_v, 1)
    load("lengths", lengths_hbm, lengths, 4 + WAVES * 16)
    barrier = pltpu.get_barrier_semaphore()
    targets = [(r, feat_at(*p)) for p in FEAT_PEERS]
    targets += [(rows_at(*p), f) for p in ROW_PEERS] + [other_core]
    for target in targets:
        pl.semaphore_signal(barrier, 1, device_id=target, device_id_type=MESH)
    for w in range(WAVES):
        for k, (which, dz, dx) in enumerate(PART_ORDER):
            row = pl.multiple_of((w * 16 + feat_at(dz, dx) * 2) * 96, 192)
            src, dst = (act, act_v) if which == "act" else (grad, grad_v)
            load(
                (w, which, dz, dx), src.at[pl.ds(row, 192)], dst.at[w, dz * 2 + dx],
                4 + w * 16 + k,
            )

    a_copies, g_copies = {}, {}
    for w in range(WAVES):
        for k, (which, dz, dx) in enumerate(PART_ORDER):
            if w == 0 and k == 0:
                loads["pin"].wait()
                loads["pout"].wait()
            loads[w, which, dz, dx].wait()
            if which == "act":
                part = jnp.dot(act_v[w, dz * 2 + dx], pin_v[...], preferred_element_type=F32)
                if dx == 0:
                    a_own[w, dz] = part
                    continue
                a_send[w, dz] = part.astype(BF16)
            else:
                part = jnp.dot(grad_v[w, dz * 2 + dx], pout_v[...], preferred_element_type=F32)
                if dz == 0:
                    g_own[w, dx] = part
                    continue
                g_send[w, dz - 1, dx] = part.astype(BF16)
                if dx == 0:
                    continue
            if w == 0 and k == 1:
                pl.semaphore_wait(barrier, len(targets))
            if which == "act":
                a_copies[w, dz] = send(
                    a_send.at[w, dz], a_recv.at[w, dz], a_ss.at[w, dz], a_rs.at[w, dz],
                    (r, feat_at(0, 1)),
                )
            else:
                g_copies[w, dz] = send(
                    g_send.at[w, dz - 1], g_recv.at[w, dz - 1], g_ss.at[w, dz], g_rs.at[w, dz],
                    (r, feat_at(dz, 0)),
                )
        if w == 0:
            load("hess", hess, hess_v, 2)
    load("train", train, train_v, 3)

    def part_stage(w):
        for dz in (2, 1, 3):
            a_copies[w, dz].wait_recv()
            a_sum[w, dz - 1] = (a_own[w, dz] + a_recv[w, dz].astype(F32)).astype(BF16)
            a_copies[w, 3 + dz] = send(
                a_sum.at[w, dz - 1], a_recv2.at[w, dz - 1],
                a_ss.at[w, 3 + dz], a_rs.at[w, 3 + dz], (r, feat_at(dz, 0)),
            )
        for dz in (2, 1, 3):
            g_copies[w, dz].wait_recv()
        g_sum[w] = (
            g_own[w, 1] + g_recv[w, 0, 1].astype(F32)
            + g_recv[w, 1, 1].astype(F32) + g_recv[w, 2, 1].astype(F32)
        ).astype(BF16)
        g_copies[w, 0] = send(
            g_sum.at[w], g_recv2.at[w], g_ss.at[w, 0], g_rs.at[w, 0], (r, feat_at(0, 1))
        )

    def kron_stage(w):
        a_copies[w, 0].wait_recv()
        for dz in (1, 2, 3):
            a_copies[w, 3 + dz].wait_recv()
        g_copies[w, 0].wait_recv()
        low_a = a_own[w, 0] + a_recv[w, 0].astype(F32)
        low_g = g_own[w, 0] + g_recv2[w].astype(F32)
        for dz in range(3):
            low_a = low_a + a_recv2[w, dz].astype(F32)
            low_g = low_g + g_recv[w, dz, 0].astype(F32)
        if w == 0:
            loads["lengths"].wait()
        token = lax.broadcasted_iota(jnp.int32, (96, 128), 0)
        for q in range(2):
            length = lengths[w * 16 + f * 2 + q]
            a = jnp.where(token < length, low_a[q * 96:(q + 1) * 96], 0.0)
            g = jnp.where(token < length, low_g[q * 96:(q + 1) * 96], 0.0)
            a_hi, g_hi = a.astype(BF16), g.astype(BF16)
            a_lo, g_lo = (a - a_hi.astype(F32)).astype(BF16), (g - g_hi.astype(F32)).astype(BF16)

            def outer(left, right):
                return lax.dot_general(
                    left, right, (((0,), (0,)), ((), ())), preferred_element_type=F32
                )

            kron = outer(g_hi, a_hi) + outer(g_hi, a_lo) + outer(g_lo, a_hi)
            kron = kron * (1.0 / jnp.sqrt(jnp.float32(96)))
            kron_send[w, :, q * 128:(q + 1) * 128] = kron.astype(BF16)
        copies = []
        for k, p in enumerate(FEAT_PEERS):
            target = feat_at(*p)
            copies.append(send(
                kron_send.at[w, pl.ds(pl.multiple_of(target * 16, 16), 16)], kron_recv.at[w, f],
                kron_ss.at[w, k], kron_rs.at[w, k], (r, target),
            ))
        kron_recv[w, f] = kron_send[w, pl.ds(pl.multiple_of(f * 16, 16), 16)]
        return copies

    def precond_stage(w, copies):
        for copy in copies:
            copy.wait_recv()
        if w == 0:
            loads["hess"].wait()
        for s in range(8):
            for q in range(2):
                kron_f32[pl.ds((s * 2 + q) * 16, 16), :] = (
                    kron_recv[w, s, :, q * 128:(q + 1) * 128].astype(F32)
                )
        for i in range(16):
            kron_lhs[:, i * 128:(i + 1) * 128] = (
                kron_f32[pl.ds(i, 16, stride=16), :].astype(BF16)
            )
        for b in range(2):
            gathered[w, r, :, b * 1024:(b + 1) * 1024] = jnp.dot(
                kron_lhs[:, b * 1024:(b + 1) * 1024], hess_v[b], preferred_element_type=F32
            ).astype(BF16)
        return [
            send(
                gathered.at[w, r], gathered.at[w, r], row_ss.at[w, k], row_rs.at[w, k],
                (rows_at(*p), f),
            )
            for k, p in enumerate(ROW_PEERS)
        ] + [forward(w, len(ROW_PEERS), r)]

    def forward(w, k, block):
        return send(
            gathered.at[w, block], gathered.at[w, block], core_ss.at[w, k], core_rs.at[w, k],
            other_core,
        )

    def gather_stage(w, copies):
        forwards = [copies[-1]]
        for k in (6, 4, 5, 2, 3, 1, 0):
            dx, dy = ROW_PEERS[k]
            copies[k].wait_recv()
            forwards.append(forward(w, k, rows_at(2 - dx, 4 - dy)))
        for copy in forwards:
            copy.wait_recv()

    def score_matmul(w, h):
        @pl.loop(0, 1024 // NTILE)
        def _(n):
            col = pl.multiple_of(n * NTILE, NTILE)
            acc = lax.dot_general(
                gathered[w].reshape(256, 2048),
                train_v[pl.ds(pl.multiple_of(h * 1024 + col, NTILE), NTILE), :],
                (((1,), (1,)), ((), ())), preferred_element_type=F32,
            )
            score_f32[w, h, :, pl.ds(col, NTILE)] = acc
            score_send[w, h, :, pl.ds(col, NTILE)] = acc.astype(BF16)

    def rows_for(target, count=32):
        return pl.ds(pl.multiple_of(target * count, count), count)

    xs, zs = {}, {}

    def score_stage(w):
        if w == 0:
            loads["train"].wait()
        score_matmul(w, 0)
        for dz in (2, 1, 3, 0):
            xs[w, dz] = send(
                score_send.at[w, 0, rows_for(feat_at(dz, 1))], x_recv.at[w, dz],
                xs_ss.at[w, dz], xs_rs.at[w, dz], (r, feat_at(0, 1)),
            )
        score_matmul(w, 1)
        for dz in (2, 1, 3):
            zs[w, dz] = send(
                score_send.at[w, 1, rows_for(lax.rem(z + dz, 4), 64)], z_recv.at[w, dz - 1],
                zs_ss.at[w, dz], zs_rs.at[w, dz], (r, feat_at(dz, 0)),
            )

    def score_stage2(w):
        for dz in (2, 1, 3):
            xs[w, dz].wait_recv()
            x_sum[w, dz - 1] = (
                score_f32[w, 0, rows_for(feat_at(dz, 0)), :] + x_recv[w, dz].astype(F32)
            ).astype(BF16)
            xs[w, 3 + dz] = send(
                x_sum.at[w, dz - 1], x_recv2.at[w, dz - 1],
                xs_ss.at[w, 3 + dz], xs_rs.at[w, 3 + dz], (r, feat_at(dz, 0)),
            )
        for dz in (2, 1, 3):
            zs[w, dz].wait_recv()
        total = score_f32[w, 1, rows_for(feat_at(0, 1)), :]
        for dz in range(3):
            total = total + z_recv[w, dz, rows_for(1 - xl), :].astype(F32)
        z_sum[w] = total.astype(BF16)
        zs[w, 0] = send(
            z_sum.at[w], z_recv2.at[w], zs_ss.at[w, 0], zs_rs.at[w, 0], (r, feat_at(0, 1))
        )

    def final_stage(w):
        xs[w, 0].wait_recv()
        for dz in (1, 2, 3):
            xs[w, 3 + dz].wait_recv()
        zs[w, 0].wait_recv()
        first = score_f32[w, 0, rows_for(f), :] + x_recv[w, 0].astype(F32)
        second = score_f32[w, 1, rows_for(f), :] + z_recv2[w].astype(F32)
        for dz in range(3):
            first = first + x_recv2[w, dz].astype(F32)
            second = second + z_recv[w, dz, rows_for(xl), :].astype(F32)
        for core in range(2):
            rows = pl.ds(core * 32 + w * 16, 16)
            out[rows, 0:1024] = first[core * 16:(core + 1) * 16] * (1.0 / 128)
            out[rows, 1024:2048] = second[core * 16:(core + 1) * 16] * (1.0 / 128)

    part_stage(0)
    part_stage(1)
    k0 = kron_stage(0)
    k1 = kron_stage(1)
    p0 = precond_stage(0, k0)
    p1 = precond_stage(1, k1)
    gather_stage(0, p0)
    score_stage(0)
    gather_stage(1, p1)
    score_stage(1)
    score_stage2(0)
    score_stage2(1)
    final_stage(0)
    final_stage(1)
    for copy in sends:
        copy.wait_send()


def on_device(activations, out_grads, proj_in, proj_out, lengths, hess_tiles, train_grads):
    hbm = pl.BlockSpec(memory_space=pl.ANY)
    n_feat, n_row = len(FEAT_PEERS), len(ROW_PEERS)
    dma = pltpu.SemaphoreType.DMA
    return pl.pallas_call(
        kernel,
        out_shape=jax.ShapeDtypeStruct((64, 2048), F32),
        in_specs=[hbm, hbm, hbm, hbm, hbm, hbm, hbm],
        out_specs=pl.BlockSpec(memory_space=pltpu.VMEM),
        scratch_shapes=[
            pltpu.SMEM((32,), jnp.int32),
            pltpu.VMEM((WAVES, 8, 192, 1024), BF16),
            pltpu.VMEM((WAVES, 8, 192, 1024), BF16),
            pltpu.VMEM((1024, 128), BF16),
            pltpu.VMEM((1024, 128), BF16),
            pltpu.VMEM((2, 1024, 1024), BF16),
            pltpu.VMEM((2048, 2048), BF16),
            pltpu.VMEM((WAVES, 4, 192, 128), BF16),
            pltpu.VMEM((WAVES, 4, 192, 128), BF16),
            pltpu.VMEM((WAVES, 4, 192, 128), F32),
            pltpu.VMEM((WAVES, 3, 192, 128), BF16),
            pltpu.VMEM((WAVES, 3, 192, 128), BF16),
            pltpu.VMEM((WAVES, 3, 2, 192, 128), BF16),
            pltpu.VMEM((WAVES, 3, 2, 192, 128), BF16),
            pltpu.VMEM((WAVES, 2, 192, 128), F32),
            pltpu.VMEM((WAVES, 192, 128), BF16),
            pltpu.VMEM((WAVES, 192, 128), BF16),
            pltpu.VMEM((WAVES, 128, 256), BF16),
            pltpu.VMEM((WAVES, 8, 16, 256), BF16),
            pltpu.VMEM((256, 128), F32),
            pltpu.VMEM((16, 2048), BF16),
            pltpu.VMEM((WAVES, 16, 16, 2048), BF16),
            pltpu.VMEM((WAVES, 2, 256, 1024), F32),
            pltpu.VMEM((WAVES, 2, 256, 1024), BF16),
            pltpu.VMEM((WAVES, 4, 32, 1024), BF16),
            pltpu.VMEM((WAVES, 3, 32, 1024), BF16),
            pltpu.VMEM((WAVES, 3, 32, 1024), BF16),
            pltpu.VMEM((WAVES, 3, 64, 1024), BF16),
            pltpu.VMEM((WAVES, 32, 1024), BF16),
            pltpu.VMEM((WAVES, 32, 1024), BF16),
            dma((5 + WAVES * 16,)),
            dma((WAVES, 7)), dma((WAVES, 7)),
            dma((WAVES, 4)), dma((WAVES, 4)),
            dma((WAVES, n_feat)), dma((WAVES, n_feat)),
            dma((WAVES, n_row)), dma((WAVES, n_row)),
            dma((WAVES, n_row + 1)), dma((WAVES, n_row + 1)),
            dma((WAVES, 7)), dma((WAVES, 7)),
            dma((WAVES, 4)), dma((WAVES, 4)),
        ],
        compiler_params=pltpu.CompilerParams(
            collective_id=0, has_side_effects=True, vmem_limit_bytes=56 * 1024 * 1024
        ),
        cost_estimate=pl.CostEstimate(
            flops=6_000_000_000, bytes_accessed=26_000_000, transcendentals=0
        ),
        name="influence",
    )(
        activations.reshape(3072, 1024), out_grads.reshape(3072, 1024),
        proj_in, proj_out, lengths, hess_tiles, train_grads,
    )


def solution(mesh):
    return jax.shard_map(
        on_device,
        mesh=mesh,
        in_specs=(
            P("rows", None, "feat"),
            P("rows", None, "feat"),
            P("feat", None),
            P("feat", None),
            P("rows"),
            P("feat", None, None),
            P("rows", "feat"),
        ),
        out_specs=P("feat", "rows"),
        check_vma=False,
    )
```

time: 87.3 us -> 64.4 us (0.74)
  Pallas kernels: 85.3 us -> 62.4 us
    pallas_call x1, Pallas kernels: 85.3 us -> 62.4 us  [on_device(): pl.pallas_call(kernel, out_shape=jax.ShapeDtypeStruct((64, 2048), F32), i...]
where the time goes in v2:
time: 64.4 us; the launch traced here: 64.2 us
  Pallas kernels  62.4 us (97%)
  local copies, waits for them, and re-layouts  1.87 us (3%)
    pallas_call x1, Pallas kernels, on_device(): pl.pallas_call(kernel, out_shape=jax.ShapeDtypeStruct((64, 2048), F32), i...  62.4 us
    unnamed x1, local copies, waits for them, and re-layouts  1.87 us

profile of v2, /device:TPU:1, one launch (start us, length us, event | category | flops | bytes accessed | tf_op | source)
XLA Modules:
  0.0 64.2 jit_solution(1184983471079121657)
XLA Ops:
  0.0 62.4 %influence.1 = f32[64,2048]{1,0:T(8,128)} custom-call(bf16[3072,1024]{1,0:T(8,128)(2,1)} %bitcast.2, bf16[3072,1024]{1,0:T(8,128)(2,1)} %bitcast.3, bf16[1024,128]{1,0:T(8,128)(2,1)} %proj_in.1, bf16[1024,128]{1,0:T(8,128)(2,1)} %proj_out.1, s32[32]{0:T(128)} %lengths_hbm.1, bf16[2,1024,1024]{2,1,0:T(8,128)(2,1)} %hess.1, bf16[2048,2048]{1,0:T(8,128)(2,1)} %train.1), custom_call_target="tpu_custom_call" | custom-call | flops 6000000000 | bytes 26000000 | tf_op jit(solution)/shard_map/influence/pallas_call | solution.py:302
  62.4 1.9 %copy.9 = f32[64,2048]{1,0:T(8,128)} copy(f32[64,2048]{1,0:T(8,128)} %influence.1) | data formatting | bytes 1048576

commit v3 on v2

--- a/solution.py
+++ b/solution.py
@@ -9,9 +9,8 @@
 BF16 = jnp.bfloat16
 F32 = jnp.float32
 WAVES = 2
-NTILE = 512
 FEAT_PEERS = [(dz, dx) for dx in (1, 0) for dz in (2, 1, 3, 0) if (dz, dx) != (0, 0)]
-ROW_PEERS = [(dx, dy) for dx in (1, 0) for dy in (2, 1, 3, 0) if (dx, dy) != (0, 0)]
+ROW_PEERS = [(1, 0), (0, 2), (0, 1), (0, 3)]
 PART_ORDER = [
     ("grad", 2, 0), ("grad", 2, 1), ("act", 2, 1), ("grad", 1, 0), ("grad", 1, 1), ("act", 1, 1),
     ("grad", 3, 0), ("grad", 3, 1), ("act", 3, 1), ("act", 0, 1),
@@ -52,20 +51,21 @@
         sends.append(copy)
         return copy
 
-    loads = {}
-
-    def load(key, src, dst, sem):
-        loads[key] = pltpu.make_async_copy(src, dst, load_sem.at[sem])
-        loads[key].start()
-
-    load("pin", proj_in, pin_v, 0)
-    load("pout", proj_out, pout_v, 1)
-    load("lengths", lengths_hbm, lengths, 4 + WAVES * 16)
     barrier = pltpu.get_barrier_semaphore()
     targets = [(r, feat_at(*p)) for p in FEAT_PEERS]
     targets += [(rows_at(*p), f) for p in ROW_PEERS] + [other_core]
     for target in targets:
         pl.semaphore_signal(barrier, 1, device_id=target, device_id_type=MESH)
+
+    loads = {}
+
+    def load(key, src, dst, sem):
+        loads[key] = pltpu.make_async_copy(src, dst, load_sem.at[sem])
+        loads[key].start()
+
+    load("pin", proj_in, pin_v, 0)
+    load("pout", proj_out, pout_v, 1)
+    load("lengths", lengths_hbm, lengths, 4 + WAVES * 16)
     for w in range(WAVES):
         for k, (which, dz, dx) in enumerate(PART_ORDER):
             row = pl.multiple_of((w * 16 + feat_at(dz, dx) * 2) * 96, 192)
@@ -98,6 +98,10 @@
                     continue
             if w == 0 and k == 1:
                 pl.semaphore_wait(barrier, len(targets))
+            if w > 0:
+                earlier = (a_copies if which == "act" else g_copies)[w - 1, dz]
+                earlier.wait_send()
+                sends[:] = [copy for copy in sends if copy is not earlier]
             if which == "act":
                 a_copies[w, dz] = send(
                     a_send.at[w, dz], a_recv.at[w, dz], a_ss.at[w, dz], a_rs.at[w, dz],
@@ -186,13 +190,11 @@
             gathered[w, r, :, b * 1024:(b + 1) * 1024] = jnp.dot(
                 kron_lhs[:, b * 1024:(b + 1) * 1024], hess_v[b], preferred_element_type=F32
             ).astype(BF16)
-        return [
-            send(
-                gathered.at[w, r], gathered.at[w, r], row_ss.at[w, k], row_rs.at[w, k],
-                (rows_at(*p), f),
-            )
-            for k, p in enumerate(ROW_PEERS)
-        ] + [forward(w, len(ROW_PEERS), r)]
+
+    def share(w, block, k, target):
+        return send(
+            gathered.at[w, block], gathered.at[w, block], row_ss.at[w, k], row_rs.at[w, k], target
+        )
 
     def forward(w, k, block):
         return send(
@@ -200,104 +202,121 @@
             other_core,
         )
 
-    def gather_stage(w, copies):
-        forwards = [copies[-1]]
-        for k in (6, 4, 5, 2, 3, 1, 0):
-            dx, dy = ROW_PEERS[k]
-            copies[k].wait_recv()
-            forwards.append(forward(w, k, rows_at(2 - dx, 4 - dy)))
+    def share_stage(w):
+        copies = {"x": share(w, r, 0, (rows_at(1, 0), f))}
+        for dy in (2, 1, 3):
+            copies[0, dy] = share(w, r, dy, (rows_at(0, dy), f))
+        return copies, [forward(w, 0, r)]
+
+    def relay_stage(w, copies, forwards):
+        copies["x"].wait_recv()
+        for dy in (2, 1, 3):
+            copies[1, dy] = share(w, rows_at(1, 0), 3 + dy, (rows_at(0, dy), f))
+        forwards.append(forward(w, 4, rows_at(1, 0)))
+
+    def gather_stage(w, copies, forwards):
+        for dx in range(2):
+            for dy in (1, 3, 2):
+                copies[dx, dy].wait_recv()
+                forwards.append(forward(w, dx * 4 + dy, rows_at(dx, 4 - dy)))
         for copy in forwards:
             copy.wait_recv()
 
-    def score_matmul(w, h):
-        @pl.loop(0, 1024 // NTILE)
-        def _(n):
-            col = pl.multiple_of(n * NTILE, NTILE)
-            acc = lax.dot_general(
-                gathered[w].reshape(256, 2048),
-                train_v[pl.ds(pl.multiple_of(h * 1024 + col, NTILE), NTILE), :],
-                (((1,), (1,)), ((), ())), preferred_element_type=F32,
-            )
-            score_f32[w, h, :, pl.ds(col, NTILE)] = acc
-            score_send[w, h, :, pl.ds(col, NTILE)] = acc.astype(BF16)
-
     def rows_for(target, count=32):
         return pl.ds(pl.multiple_of(target * count, count), count)
+
+    def score_matmul(w, block):
+        acc = lax.dot_general(
+            gathered[w].reshape(256, 2048), train_v[block * 512:(block + 1) * 512, :],
+            (((1,), (1,)), ((), ())), preferred_element_type=F32,
+        )
+        score_f32[w, block] = acc
+        score_send[w, block] = acc.astype(BF16)
 
     xs, zs = {}, {}
 
     def score_stage(w):
         if w == 0:
             loads["train"].wait()
-        score_matmul(w, 0)
-        for dz in (2, 1, 3, 0):
-            xs[w, dz] = send(
-                score_send.at[w, 0, rows_for(feat_at(dz, 1))], x_recv.at[w, dz],
-                xs_ss.at[w, dz], xs_rs.at[w, dz], (r, feat_at(0, 1)),
-            )
-        score_matmul(w, 1)
+        for s in range(2):
+            score_matmul(w, s)
+            for dz in (2, 1, 3, 0):
+                xs[w, s, dz] = send(
+                    score_send.at[w, s, rows_for(feat_at(dz, 1))], x_recv.at[w, s, dz],
+                    xs_ss.at[w, s, dz], xs_rs.at[w, s, dz], (r, feat_at(0, 1)),
+                )
+            score_matmul(w, 2 + s)
+            for dz in (2, 1, 3):
+                zs[w, s, dz] = send(
+                    score_send.at[w, 2 + s, rows_for(lax.rem(z + dz, 4), 64)],
+                    z_recv.at[w, s, dz - 1],
+                    zs_ss.at[w, s, dz], zs_rs.at[w, s, dz], (r, feat_at(dz, 0)),
+                )
+
+    def score_stage2(w, s):
         for dz in (2, 1, 3):
-            zs[w, dz] = send(
-                score_send.at[w, 1, rows_for(lax.rem(z + dz, 4), 64)], z_recv.at[w, dz - 1],
-                zs_ss.at[w, dz], zs_rs.at[w, dz], (r, feat_at(dz, 0)),
-            )
-
-    def score_stage2(w):
-        for dz in (2, 1, 3):
-            xs[w, dz].wait_recv()
-            x_sum[w, dz - 1] = (
-                score_f32[w, 0, rows_for(feat_at(dz, 0)), :] + x_recv[w, dz].astype(F32)
+            xs[w, s, dz].wait_recv()
+            x_sum[w, s, dz - 1] = (
+                score_f32[w, s, rows_for(feat_at(dz, 0)), :] + x_recv[w, s, dz].astype(F32)
             ).astype(BF16)
-            xs[w, 3 + dz] = send(
-                x_sum.at[w, dz - 1], x_recv2.at[w, dz - 1],
-                xs_ss.at[w, 3 + dz], xs_rs.at[w, 3 + dz], (r, feat_at(dz, 0)),
+            xs[w, s, 3 + dz] = send(
+                x_sum.at[w, s, dz - 1], x_recv2.at[w, s, dz - 1],
+                xs_ss.at[w, s, 3 + dz], xs_rs.at[w, s, 3 + dz], (r, feat_at(dz, 0)),
             )
         for dz in (2, 1, 3):
-            zs[w, dz].wait_recv()
-        total = score_f32[w, 1, rows_for(feat_at(0, 1)), :]
+            zs[w, s, dz].wait_recv()
+        total = score_f32[w, 2 + s, rows_for(feat_at(0, 1)), :]
         for dz in range(3):
-            total = total + z_recv[w, dz, rows_for(1 - xl), :].astype(F32)
-        z_sum[w] = total.astype(BF16)
-        zs[w, 0] = send(
-            z_sum.at[w], z_recv2.at[w], zs_ss.at[w, 0], zs_rs.at[w, 0], (r, feat_at(0, 1))
-        )
-
-    def final_stage(w):
-        xs[w, 0].wait_recv()
+            total = total + z_recv[w, s, dz, rows_for(1 - xl), :].astype(F32)
+        z_sum[w, s] = total.astype(BF16)
+        zs[w, s, 0] = send(
+            z_sum.at[w, s], z_recv2.at[w, s], zs_ss.at[w, s, 0], zs_rs.at[w, s, 0],
+            (r, feat_at(0, 1)),
+        )
+
+    def final_stage(w, s):
+        xs[w, s, 0].wait_recv()
         for dz in (1, 2, 3):
-            xs[w, 3 + dz].wait_recv()
-        zs[w, 0].wait_recv()
-        first = score_f32[w, 0, rows_for(f), :] + x_recv[w, 0].astype(F32)
-        second = score_f32[w, 1, rows_for(f), :] + z_recv2[w].astype(F32)
+            xs[w, s, 3 + dz].wait_recv()
+        zs[w, s, 0].wait_recv()
+        first = score_f32[w, s, rows_for(f), :] + x_recv[w, s, 0].astype(F32)
+        second = score_f32[w, 2 + s, rows_for(f), :] + z_recv2[w, s].astype(F32)
         for dz in range(3):
-            first = first + x_recv2[w, dz].astype(F32)
-            second = second + z_recv[w, dz, rows_for(xl), :].astype(F32)
+            first = first + x_recv2[w, s, dz].astype(F32)
+            second = second + z_recv[w, s, dz, rows_for(xl), :].astype(F32)
         for core in range(2):
             rows = pl.ds(core * 32 + w * 16, 16)
-            out[rows, 0:1024] = first[core * 16:(core + 1) * 16] * (1.0 / 128)
-            out[rows, 1024:2048] = second[core * 16:(core + 1) * 16] * (1.0 / 128)
+            half = slice(core * 16, (core + 1) * 16)
+            out[rows, s * 512:(s + 1) * 512] = first[half] * (1.0 / 128)
+            out[rows, 1024 + s * 512:1536 + s * 512] = second[half] * (1.0 / 128)
 
     part_stage(0)
+    k0 = kron_stage(0)
     part_stage(1)
-    k0 = kron_stage(0)
+    precond_stage(0, k0)
+    g0 = share_stage(0)
     k1 = kron_stage(1)
-    p0 = precond_stage(0, k0)
-    p1 = precond_stage(1, k1)
-    gather_stage(0, p0)
+    precond_stage(1, k1)
+    relay_stage(0, *g0)
+    g1 = share_stage(1)
+    relay_stage(1, *g1)
+    gather_stage(0, *g0)
     score_stage(0)
-    gather_stage(1, p1)
+    gather_stage(1, *g1)
     score_stage(1)
-    score_stage2(0)
-    score_stage2(1)
-    final_stage(0)
-    final_stage(1)
+    for w in range(WAVES):
+        for s in range(2):
+            score_stage2(w, s)
+    for w in range(WAVES):
+        for s in range(2):
+            final_stage(w, s)
     for copy in sends:
         copy.wait_send()
 
 
 def on_device(activations, out_grads, proj_in, proj_out, lengths, hess_tiles, train_grads):
     hbm = pl.BlockSpec(memory_space=pl.ANY)
-    n_feat, n_row = len(FEAT_PEERS), len(ROW_PEERS)
+    n_feat = len(FEAT_PEERS)
     dma = pltpu.SemaphoreType.DMA
     return pl.pallas_call(
         kernel,
@@ -327,22 +346,22 @@
             pltpu.VMEM((256, 128), F32),
             pltpu.VMEM((16, 2048), BF16),
             pltpu.VMEM((WAVES, 16, 16, 2048), BF16),
-            pltpu.VMEM((WAVES, 2, 256, 1024), F32),
-            pltpu.VMEM((WAVES, 2, 256, 1024), BF16),
-            pltpu.VMEM((WAVES, 4, 32, 1024), BF16),
-            pltpu.VMEM((WAVES, 3, 32, 1024), BF16),
-            pltpu.VMEM((WAVES, 3, 32, 1024), BF16),
-            pltpu.VMEM((WAVES, 3, 64, 1024), BF16),
-            pltpu.VMEM((WAVES, 32, 1024), BF16),
-            pltpu.VMEM((WAVES, 32, 1024), BF16),
+            pltpu.VMEM((WAVES, 4, 256, 512), F32),
+            pltpu.VMEM((WAVES, 4, 256, 512), BF16),
+            pltpu.VMEM((WAVES, 2, 4, 32, 512), BF16),
+            pltpu.VMEM((WAVES, 2, 3, 32, 512), BF16),
+            pltpu.VMEM((WAVES, 2, 3, 32, 512), BF16),
+            pltpu.VMEM((WAVES, 2, 3, 64, 512), BF16),
+            pltpu.VMEM((WAVES, 2, 32, 512), BF16),
+            pltpu.VMEM((WAVES, 2, 32, 512), BF16),
             dma((5 + WAVES * 16,)),
             dma((WAVES, 7)), dma((WAVES, 7)),
             dma((WAVES, 4)), dma((WAVES, 4)),
             dma((WAVES, n_feat)), dma((WAVES, n_feat)),
-            dma((WAVES, n_row)), dma((WAVES, n_row)),
-            dma((WAVES, n_row + 1)), dma((WAVES, n_row + 1)),
             dma((WAVES, 7)), dma((WAVES, 7)),
-            dma((WAVES, 4)), dma((WAVES, 4)),
+            dma((WAVES, 8)), dma((WAVES, 8)),
+            dma((WAVES, 2, 7)), dma((WAVES, 2, 7)),
+            dma((WAVES, 2, 4)), dma((WAVES, 2, 4)),
         ],
         compiler_params=pltpu.CompilerParams(
             collective_id=0, has_side_effects=True, vmem_limit_bytes=56 * 1024 * 1024

time: 64.4 us -> 62.8 us (0.975)
  Pallas kernels: 62.4 us -> 60.8 us
    pallas_call x1, Pallas kernels: 62.4 us -> 60.8 us  [on_device(): pl.pallas_call(kernel, out_shape=jax.ShapeDtypeStruct((64, 2048), F32), i...]
where the time goes in v3:
time: 62.8 us; the launch traced here: 62.7 us
  Pallas kernels  60.8 us (97%)
  local copies, waits for them, and re-layouts  1.87 us (3%)
    pallas_call x1, Pallas kernels, on_device(): pl.pallas_call(kernel, out_shape=jax.ShapeDtypeStruct((64, 2048), F32), i...  60.8 us
    unnamed x1, local copies, waits for them, and re-layouts  1.87 us

profile of v3, /device:TPU:1, one launch (start us, length us, event | category | flops | bytes accessed | tf_op | source)
XLA Modules:
  0.0 62.7 jit_solution(10177172671778397074)
XLA Ops:
  0.0 60.8 %influence.1 = f32[64,2048]{1,0:T(8,128)} custom-call(bf16[3072,1024]{1,0:T(8,128)(2,1)} %bitcast.2, bf16[3072,1024]{1,0:T(8,128)(2,1)} %bitcast.3, bf16[1024,128]{1,0:T(8,128)(2,1)} %proj_in.1, bf16[1024,128]{1,0:T(8,128)(2,1)} %proj_out.1, s32[32]{0:T(128)} %lengths_hbm.1, bf16[2,1024,1024]{2,1,0:T(8,128)(2,1)} %hess.1, bf16[2048,2048]{1,0:T(8,128)(2,1)} %train.1), custom_call_target="tpu_custom_call" | custom-call | flops 6000000000 | bytes 26000000 | tf_op jit(solution)/shard_map/influence/pallas_call | solution.py:321
  60.8 1.9 %copy.9 = f32[64,2048]{1,0:T(8,128)} copy(f32[64,2048]{1,0:T(8,128)} %influence.1) | data formatting | bytes 1048576

commit v4 on v3

--- a/solution.py
+++ b/solution.py
@@ -9,6 +9,7 @@
 BF16 = jnp.bfloat16
 F32 = jnp.float32
 WAVES = 2
+X_ROWS = (512, 768)
 FEAT_PEERS = [(dz, dx) for dx in (1, 0) for dz in (2, 1, 3, 0) if (dz, dx) != (0, 0)]
 ROW_PEERS = [(1, 0), (0, 2), (0, 1), (0, 3)]
 PART_ORDER = [
@@ -225,53 +226,64 @@
     def rows_for(target, count=32):
         return pl.ds(pl.multiple_of(target * count, count), count)
 
+    starts, widths = [0] * 4, [X_ROWS[0], X_ROWS[1], 1024 - X_ROWS[0], 1024 - X_ROWS[1]]
+    for block, before in ((2, 0), (1, 2), (3, 1)):
+        starts[block] = starts[before] + widths[before]
+    parts = [pl.ds(0, width) for width in widths]
+    xs, zs = {}, {}
+
     def score_matmul(w, block):
         acc = lax.dot_general(
-            gathered[w].reshape(256, 2048), train_v[block * 512:(block + 1) * 512, :],
+            gathered[w].reshape(256, 2048),
+            train_v[starts[block]:starts[block] + widths[block], :],
             (((1,), (1,)), ((), ())), preferred_element_type=F32,
         )
-        score_f32[w, block] = acc
-        score_send[w, block] = acc.astype(BF16)
-
-    xs, zs = {}, {}
+        score_f32[w, block, :, parts[block]] = acc
+        score_send[w, block, :, parts[block]] = acc.astype(BF16)
 
     def score_stage(w):
         if w == 0:
             loads["train"].wait()
         for s in range(2):
             score_matmul(w, s)
+            part = parts[s]
             for dz in (2, 1, 3, 0):
                 xs[w, s, dz] = send(
-                    score_send.at[w, s, rows_for(feat_at(dz, 1))], x_recv.at[w, s, dz],
+                    score_send.at[w, s, rows_for(feat_at(dz, 1)), part],
+                    x_recv.at[w, s, dz, :, part],
                     xs_ss.at[w, s, dz], xs_rs.at[w, s, dz], (r, feat_at(0, 1)),
                 )
             score_matmul(w, 2 + s)
+            part = parts[2 + s]
             for dz in (2, 1, 3):
                 zs[w, s, dz] = send(
-                    score_send.at[w, 2 + s, rows_for(lax.rem(z + dz, 4), 64)],
-                    z_recv.at[w, s, dz - 1],
+                    score_send.at[w, 2 + s, rows_for(lax.rem(z + dz, 4), 64), part],
+                    z_recv.at[w, s, dz - 1, :, part],
                     zs_ss.at[w, s, dz], zs_rs.at[w, s, dz], (r, feat_at(dz, 0)),
                 )
 
     def score_stage2(w, s):
+        part = parts[s]
         for dz in (2, 1, 3):
             xs[w, s, dz].wait_recv()
-            x_sum[w, s, dz - 1] = (
-                score_f32[w, s, rows_for(feat_at(dz, 0)), :] + x_recv[w, s, dz].astype(F32)
+            x_sum[w, s, dz - 1, :, part] = (
+                score_f32[w, s, rows_for(feat_at(dz, 0)), part]
+                + x_recv[w, s, dz, :, part].astype(F32)
             ).astype(BF16)
             xs[w, s, 3 + dz] = send(
-                x_sum.at[w, s, dz - 1], x_recv2.at[w, s, dz - 1],
+                x_sum.at[w, s, dz - 1, :, part], x_recv2.at[w, s, dz - 1, :, part],
                 xs_ss.at[w, s, 3 + dz], xs_rs.at[w, s, 3 + dz], (r, feat_at(dz, 0)),
             )
+        part = parts[2 + s]
         for dz in (2, 1, 3):
             zs[w, s, dz].wait_recv()
-        total = score_f32[w, 2 + s, rows_for(feat_at(0, 1)), :]
+        total = score_f32[w, 2 + s, rows_for(feat_at(0, 1)), part]
         for dz in range(3):
-            total = total + z_recv[w, s, dz, rows_for(1 - xl), :].astype(F32)
-        z_sum[w, s] = total.astype(BF16)
+            total = total + z_recv[w, s, dz, rows_for(1 - xl), part].astype(F32)
+        z_sum[w, s, :, part] = total.astype(BF16)
         zs[w, s, 0] = send(
-            z_sum.at[w, s], z_recv2.at[w, s], zs_ss.at[w, s, 0], zs_rs.at[w, s, 0],
-            (r, feat_at(0, 1)),
+            z_sum.at[w, s, :, part], z_recv2.at[w, s, :, part],
+            zs_ss.at[w, s, 0], zs_rs.at[w, s, 0], (r, feat_at(0, 1)),
         )
 
     def final_stage(w, s):
@@ -279,16 +291,17 @@
         for dz in (1, 2, 3):
             xs[w, s, 3 + dz].wait_recv()
         zs[w, s, 0].wait_recv()
-        first = score_f32[w, s, rows_for(f), :] + x_recv[w, s, 0].astype(F32)
-        second = score_f32[w, 2 + s, rows_for(f), :] + z_recv2[w, s].astype(F32)
+        part, part2 = parts[s], parts[2 + s]
+        first = score_f32[w, s, rows_for(f), part] + x_recv[w, s, 0, :, part].astype(F32)
+        second = score_f32[w, 2 + s, rows_for(f), part2] + z_recv2[w, s, :, part2].astype(F32)
         for dz in range(3):
-            first = first + x_recv2[w, s, dz].astype(F32)
-            second = second + z_recv[w, s, dz, rows_for(xl), :].astype(F32)
+            first = first + x_recv2[w, s, dz, :, part].astype(F32)
+            second = second + z_recv[w, s, dz, rows_for(xl), part2].astype(F32)
         for core in range(2):
             rows = pl.ds(core * 32 + w * 16, 16)
             half = slice(core * 16, (core + 1) * 16)
-            out[rows, s * 512:(s + 1) * 512] = first[half] * (1.0 / 128)
-            out[rows, 1024 + s * 512:1536 + s * 512] = second[half] * (1.0 / 128)
+            out[rows, pl.ds(starts[s], widths[s])] = first[half] * (1.0 / 128)
+            out[rows, pl.ds(starts[2 + s], widths[2 + s])] = second[half] * (1.0 / 128)
 
     part_stage(0)
     k0 = kron_stage(0)
@@ -346,14 +359,14 @@
             pltpu.VMEM((256, 128), F32),
             pltpu.VMEM((16, 2048), BF16),
             pltpu.VMEM((WAVES, 16, 16, 2048), BF16),
-            pltpu.VMEM((WAVES, 4, 256, 512), F32),
-            pltpu.VMEM((WAVES, 4, 256, 512), BF16),
-            pltpu.VMEM((WAVES, 2, 4, 32, 512), BF16),
-            pltpu.VMEM((WAVES, 2, 3, 32, 512), BF16),
-            pltpu.VMEM((WAVES, 2, 3, 32, 512), BF16),
-            pltpu.VMEM((WAVES, 2, 3, 64, 512), BF16),
-            pltpu.VMEM((WAVES, 2, 32, 512), BF16),
-            pltpu.VMEM((WAVES, 2, 32, 512), BF16),
+            pltpu.VMEM((WAVES, 4, 256, 768), F32),
+            pltpu.VMEM((WAVES, 4, 256, 768), BF16),
+            pltpu.VMEM((WAVES, 2, 4, 32, 768), BF16),
+            pltpu.VMEM((WAVES, 2, 3, 32, 768), BF16),
+            pltpu.VMEM((WAVES, 2, 3, 32, 768), BF16),
+            pltpu.VMEM((WAVES, 2, 3, 64, 768), BF16),
+            pltpu.VMEM((WAVES, 2, 32, 768), BF16),
+            pltpu.VMEM((WAVES, 2, 32, 768), BF16),
             dma((5 + WAVES * 16,)),
             dma((WAVES, 7)), dma((WAVES, 7)),
             dma((WAVES, 4)), dma((WAVES, 4)),

time: 62.8 us -> 62.3 us (level)
  no operation moved by 1% of the time
where the time goes in v4:
time: 62.3 us; the launch traced here: 62.2 us
  Pallas kernels  60.3 us (97%)
  local copies, waits for them, and re-layouts  1.87 us (3%)
    pallas_call x1, Pallas kernels, on_device(): pl.pallas_call(kernel, out_shape=jax.ShapeDtypeStruct((64, 2048), F32), i...  60.3 us
    unnamed x1, local copies, waits for them, and re-layouts  1.87 us

profile of v4, /device:TPU:1, one launch (start us, length us, event | category | flops | bytes accessed | tf_op | source)
XLA Modules:
  0.0 62.2 jit_solution(7978177644985905714)
XLA Ops:
  0.0 60.3 %influence.1 = f32[64,2048]{1,0:T(8,128)} custom-call(bf16[3072,1024]{1,0:T(8,128)(2,1)} %bitcast.2, bf16[3072,1024]{1,0:T(8,128)(2,1)} %bitcast.3, bf16[1024,128]{1,0:T(8,128)(2,1)} %proj_in.1, bf16[1024,128]{1,0:T(8,128)(2,1)} %proj_out.1, s32[32]{0:T(128)} %lengths_hbm.1, bf16[2,1024,1024]{2,1,0:T(8,128)(2,1)} %hess.1, bf16[2048,2048]{1,0:T(8,128)(2,1)} %train.1), custom_call_target="tpu_custom_call" | custom-call | flops 6000000000 | bytes 26000000 | tf_op jit(solution)/shard_map/influence/pallas_call | solution.py:334
  60.3 1.9 %copy.9 = f32[64,2048]{1,0:T(8,128)} copy(f32[64,2048]{1,0:T(8,128)} %influence.1) | data formatting | bytes 1048576

commit v5 on v4

--- a/solution.py
+++ b/solution.py
@@ -356,7 +356,7 @@
             pltpu.VMEM((WAVES, 192, 128), BF16),
             pltpu.VMEM((WAVES, 128, 256), BF16),
             pltpu.VMEM((WAVES, 8, 16, 256), BF16),
-            pltpu.VMEM((256, 128), F32),
+            pltpu.VMEM((272, 128), F32),
             pltpu.VMEM((16, 2048), BF16),
             pltpu.VMEM((WAVES, 16, 16, 2048), BF16),
             pltpu.VMEM((WAVES, 4, 256, 768), F32),

time: 62.3 us -> 62.3 us (level)
  no operation moved by 1% of the time
where the time goes in v5:
time: 62.3 us; the launch traced here: 62.2 us
  Pallas kernels  60.3 us (97%)
  local copies, waits for them, and re-layouts  1.87 us (3%)
    pallas_call x1, Pallas kernels, on_device(): pl.pallas_call(kernel, out_shape=jax.ShapeDtypeStruct((64, 2048), F32), i...  60.3 us
    unnamed x1, local copies, waits for them, and re-layouts  1.87 us

profile of v5, /device:TPU:1, one launch (start us, length us, event | category | flops | bytes accessed | tf_op | source)
XLA Modules:
  0.0 62.2 jit_solution(11170300176154242440)
XLA Ops:
  0.0 60.3 %influence.1 = f32[64,2048]{1,0:T(8,128)} custom-call(bf16[3072,1024]{1,0:T(8,128)(2,1)} %bitcast.2, bf16[3072,1024]{1,0:T(8,128)(2,1)} %bitcast.3, bf16[1024,128]{1,0:T(8,128)(2,1)} %proj_in.1, bf16[1024,128]{1,0:T(8,128)(2,1)} %proj_out.1, s32[32]{0:T(128)} %lengths_hbm.1, bf16[2,1024,1024]{2,1,0:T(8,128)(2,1)} %hess.1, bf16[2048,2048]{1,0:T(8,128)(2,1)} %train.1), custom_call_target="tpu_custom_call" | custom-call | flops 6000000000 | bytes 26000000 | tf_op jit(solution)/shard_map/influence/pallas_call | solution.py:334
  60.3 1.9 %copy.9 = f32[64,2048]{1,0:T(8,128)} copy(f32[64,2048]{1,0:T(8,128)} %influence.1) | data formatting | bytes 1048576
